TPU v7x, 256 devices: a whole 4x4x8 slice. The times are simulated.
256 devices in a mesh: row: 16 (over z_lo, y), col: 16 (over x, z_hi, core).
Axes of the slice: x: 4, y: 4, z: 8 (z_hi: 2, z_lo: 4; z = z_hi * 4 + z_lo), core: 2. Of those that a mesh axis runs over, the one named last changes fastest.
Arguments:
- b_factors: bfloat16 [3, 6144, 8192], P(None, ('row', 'col')), may hold values from -1.5 to 1.5
- occ_energy: int32 [1536], replicated, may hold values from -2048 to -256
- vir_energy: int32 [6144], P(('row', 'col')), may hold values from 128 to 8192
- pair_ids: int32 [3], replicated, may hold values from 0 to 1535
Outputs:
- gamma: float32 [3, 6144, 8192], P(None, ('row', 'col'))
- density: float32 [6144, 384], P(('row', 'col'))
All inputs are finite; a program needn't handle non-finite values.
Results may differ from a plain program's by a relative error of at most 0.0021.
Values may be sent and summed in bfloat16 or wider, within the bound.
A program may use at most 128 MiB of HBM per device.

v0:
```python
import jax
import jax.numpy as jnp
from jax import lax
from jax.sharding import PartitionSpec as P


def shards(b_factors, occ_energy, vir_energy, pair_ids):
    occ = occ_energy.astype(jnp.float32) / 1024.0
    positions = jnp.arange(occ_energy.shape[0], dtype=jnp.int32)
    picked = jnp.sum(jnp.where(positions[None, :] == pair_ids[:, None], occ[None, :], 0.0), axis=1)
    pair_count = b_factors.shape[0] - 1
    contract = (((1,), (1,)), ((), ()))
    a_panel, a_level = (
        lax.all_gather(b_factors[0], "col", axis=0, tiled=True),
        lax.all_gather(vir_energy, "col", axis=0, tiled=True),
    )
    b_panels, b_level = (
        lax.all_gather(b_factors[1:], "row", axis=1, tiled=True),
        lax.all_gather(vir_energy, "row", axis=0, tiled=True),
    )
    a_energy = a_level.astype(jnp.float32) / 1024.0
    b_energy = b_level.astype(jnp.float32) / 1024.0
    amplitudes = []
    for k in range(pair_count):
        shift = picked[0] + picked[1 + k]
        integral = lax.dot_general(
            a_panel, b_panels[k], contract, preferred_element_type=jnp.float32
        )
        amplitudes.append(
            (integral / (shift - a_energy[:, None] - b_energy[None, :])).astype(jnp.bfloat16)
        )
    total = None
    for term_k in range(pair_count):
        slab = amplitudes[term_k]
        term_product = jnp.dot(slab, b_panels[term_k], preferred_element_type=jnp.float32)
        total = term_product if total is None else total + term_product
    gamma_first = lax.psum_scatter(total, "col", scatter_dimension=0, tiled=True)
    seconds = []
    for k in range(pair_count):
        cols = amplitudes[k]
        seconds.append(
            lax.psum_scatter(
                lax.dot_general(
                    cols, a_panel, (((0,), (0,)), ((), ())), preferred_element_type=jnp.float32
                ),
                "row",
                scatter_dimension=0,
                tiled=True,
            )
        )
    gamma_second = jnp.stack(seconds)
    dens_part = None
    for k in range(pair_count):
        product = lax.dot_general(
            amplitudes[k], amplitudes[k], contract, preferred_element_type=jnp.float32
        )
        dens_part = product if dens_part is None else dens_part + product
    density = lax.psum_scatter(dens_part, "col", scatter_dimension=0, tiled=True)
    gamma = jnp.concatenate([gamma_first[None], gamma_second], axis=0)
    return (gamma, density)


def solution(mesh):
    in_specs = (P(None, ("row", "col"), None), P(), P(("row", "col")), P())
    out_specs = (P(None, ("row", "col"), None), P(("row", "col"), None))
    return jax.shard_map(shards, mesh=mesh, in_specs=in_specs, out_specs=out_specs, check_vma=False)
```

profile of v0, /device:TPU:33, one launch (start us, length us, event | category | flops | bytes accessed | tf_op | source)
XLA Modules:
  0.0 820.7 jit_solution(15189010398965634728)
XLA Ops:
  7.2 0.0 all-gather.6.cloned.1.call-start
  7.2 1.8 slice.24
  9.0 0.0 all-gather.6.cloned.1.call-update
  9.0 0.0 all-gather.4.cloned.1.call-start
  9.1 2.1 slice.25
  11.1 0.0 all-gather.4.cloned.1.call-update
  11.2 0.0 reduce-scatter.7.cloned.1.call-start
  11.2 0.7 convert_multiply_fusion
  11.9 0.8 select_reduce_fusion
  12.8 0.6 fusion.23
  15.8 1.3 dynamic-slice
  17.1 1.3 dynamic-slice.1
  19.6 0.9 dynamic-update-slice
  20.5 0.8 dynamic-update-slice.1
  21.3 15.6 %all-reduce = s32[384]{0:T(512)S(1)} all-reduce(s32[384]{0:T(512)S(1)} %dynamic-update-slice), channel_id=1, replica_groups=mesh['row'=16,'col'=16] {'col'}, use_global_device_ids=true, to_apply=%add | all-reduce | flops 384 | bytes 3072
  36.9 11.6 %all-reduce.1 = s32[384]{0:T(512)S(1)} all-reduce(s32[384]{0:T(512)S(1)} %dynamic-update-slice.1), channel_id=1, replica_groups=mesh['row'=16,'col'=16] {'row'}, use_global_device_ids=true, to_apply=%add.1 | all-reduce | flops 384 | bytes 3072
  48.5 57.3 %all-gather.6.cloned.1.call-done = bf16[1,384,8192]{2,1,0:T(8,128)(2,1)} async-done(((bf16[1,24,8192]{2,1,0:T(8,128)(2,1)}), bf16[1,384,8192]{2,1,0:T(8,128)(2,1)}) %all-gather.6.cloned.1.call-update) | async-done | bytes 6291472 | tf_op jit(solution)/shard_map/all_gather | solution.py:14
  105.8 139.6 %all-gather.4.cloned.1.call-done = bf16[2,384,8192]{2,1,0:T(8,128)(2,1)} async-done(((bf16[2,24,8192]{2,1,0:T(8,128)(2,1)}), bf16[2,384,8192]{2,1,0:T(8,128)(2,1)}) %all-gather.4.cloned.1.call-update) | async-done | bytes 12582928 | tf_op jit(solution)/shard_map/all_gather | solution.py:18
  245.5 8.0 fusion.12
  253.5 0.0 copy-start
  253.5 5.7 fusion.8
  259.2 0.0 copy-done
  259.2 6.2 fusion.18
  265.4 9.3 %convolution_add_fusion = f32[384,8192]{1,0:T(8,128)} fusion(f32[384,8192]{1,0:T(8,128)S(1)} %fusion.8, bf16[384,384]{1,0:T(8,128)(2,1)S(1)} %fusion.18, bf16[2,384,8192]{2,1,0:T(8,128)(2,1)} %all-gather.4.cloned.1.call-done), kind=kOutput, calls=%fused_computation | convolution fusion | flops 2419064832 | bytes 31752192 | tf_op jit(solution)/shard_map/dot_general | solution.py:35
  274.7 0.0 reduce-scatter.7.cloned.1.call-update
  274.7 0.2 reduce-scatter.9.cloned.1.call-start
  275.0 10.9 %fusion.2 = f32[384,8192]{1,0:T(8,128)} fusion(bf16[384,384]{1,0:T(8,128)(2,1)S(1)} %fusion.12, bf16[1,384,8192]{2,1,0:T(8,128)(2,1)} %all-gather.6.cloned.1.call-done), kind=kOutput, calls=%fused_computation.5 | convolution fusion | flops 2415919104 | bytes 19169280 | tf_op jit(solution)/shard_map/dot_general | solution.py:43
  285.8 0.0 reduce-scatter.9.cloned.1.call-update
  285.9 0.0 reduce-scatter.11.cloned.1.call-start
  285.9 12.8 %fusion = f32[384,8192]{1,0:T(8,128)} fusion(bf16[384,384]{1,0:T(8,128)(2,1)S(1)} %fusion.18, bf16[1,384,8192]{2,1,0:T(8,128)(2,1)} %all-gather.6.cloned.1.call-done), kind=kOutput, calls=%fused_computation.3 | convolution fusion | flops 2415919104 | bytes 19169280 | tf_op jit(solution)/shard_map/dot_general | solution.py:43
  298.8 0.0 reduce-scatter.11.cloned.1.call-update
  298.8 0.0 reduce-scatter.13.cloned.1.call-start
  298.8 0.3 fusion.24
  299.2 1.2 convolution_add_fusion.1
  300.4 0.0 reduce-scatter.13.cloned.1.call-update
  300.4 150.1 %reduce-scatter.7.cloned.1.call-done = f32[24,8192]{1,0:T(8,128)} async-done(((f32[384,8192]{1,0:T(8,128)}), f32[24,8192]{1,0:T(8,128)}) %reduce-scatter.7.cloned.1.call-update) | async-done | bytes 786448 | tf_op jit(solution)/shard_map/reduce_scatter | solution.py:37
  450.5 141.1 %reduce-scatter.9.cloned.1.call-done = f32[24,8192]{1,0:T(8,128)} async-done(((f32[384,8192]{1,0:T(8,128)}), f32[24,8192]{1,0:T(8,128)}) %reduce-scatter.9.cloned.1.call-update) | async-done | bytes 786448 | tf_op jit(solution)/shard_map/reduce_scatter | solution.py:42
  591.6 144.3 %reduce-scatter.11.cloned.1.call-done = f32[24,8192]{1,0:T(8,128)} async-done(((f32[384,8192]{1,0:T(8,128)}), f32[24,8192]{1,0:T(8,128)}) %reduce-scatter.11.cloned.1.call-update) | async-done | bytes 786448 | tf_op jit(solution)/shard_map/reduce_scatter | solution.py:42
  735.9 3.2 pad_maximum_fusion
  739.1 74.8 %reduce-scatter.13.cloned.1.call-done = f32[24,384]{1,0:T(8,128)} async-done(((f32[384,384]{1,0:T(8,128)}), f32[24,384]{1,0:T(8,128)}) %reduce-scatter.13.cloned.1.call-update) | async-done | bytes 36880
  (4 shorter events, 0.0 us)
Async XLA Ops:
  7.2 98.7 %all-gather.6.cloned.1.call-start = ((), (), s32[]{:S(2)}) async-start(), calls=%async_computation.8 | async-start | bytes 6684672 | tf_op jit(solution)/shard_map/all_gather | solution.py:14
  9.0 236.5 %all-gather.4.cloned.1.call-start = ((), (), s32[]{:S(2)}) async-start(), calls=%async_computation.4 | async-start | bytes 13369344 | tf_op jit(solution)/shard_map/all_gather | solution.py:18
  11.2 439.3 %reduce-scatter.7.cloned.1.call-start = ((), (), s32[]{:S(2)}) async-start(), calls=%async_computation.5 | async-start | bytes 13369344 | tf_op jit(solution)/shard_map/reduce_scatter | solution.py:37
  253.5 5.7 copy-start
  274.7 316.9 %reduce-scatter.9.cloned.1.call-start = ((), (), s32[]{:S(2)}) async-start(), calls=%async_computation.6 | async-start | bytes 13369344 | tf_op jit(solution)/shard_map/reduce_scatter | solution.py:42
  285.9 450.0 %reduce-scatter.11.cloned.1.call-start = ((), (), s32[]{:S(2)}) async-start(), calls=%async_computation.7 | async-start | bytes 13369344 | tf_op jit(solution)/shard_map/reduce_scatter | solution.py:42
  298.8 515.0 %reduce-scatter.13.cloned.1.call-start = ((), (), s32[]{:S(2)}) async-start(), calls=%async_computation.9 | async-start | bytes 626688
Sparse Core Ops, SparseCore 0:
  10.7 95.1 all-gather.5
  108.2 137.2 all-gather.3
  274.9 175.5 reduce-scatter.6
  453.1 138.4 reduce-scatter.8
  594.2 141.6 reduce-scatter.10
  740.9 72.8 reduce-scatter.12
where the time goes:
time: 824 us; the launch traced here: 821 us
  waiting for transfers between devices  707 us (86%)
  matrix products  54.5 us (7%)
  blocking collectives  27.2 us (3%)
  between operations  17.9 us (2%)
  local copies, waits for them, and re-layouts  8.71 us (1%)
    reduce_scatter x2, waiting for transfers between devices, shards(): lax.psum_scatter(lax.dot_general(cols, a_panel, (((0,), (0,)), ((), ())),...  285 us
    reduce_scatter x1, waiting for transfers between devices, shards(): lax.psum_scatter(total, 'col', scatter_dimension=0, tiled=True)  150 us
    all_gather x1, waiting for transfers between devices, shards(): lax.all_gather(b_factors[1:], 'row', axis=1, tiled=True)  140 us
    unnamed x7, waiting for transfers between devices  74.9 us
    all_gather x1, waiting for transfers between devices, shards(): lax.all_gather(b_factors[0], 'col', axis=0, tiled=True)  57.3 us
    unnamed x2, blocking collectives  27.2 us
    dot_general x2, matrix products, shards(): lax.dot_general(cols, a_panel, (((0,), (0,)), ((), ())), preferred_elemen...  23.7 us
  transfers between devices with their start and end apart: 6, of which 6 were waited for; matrix products, arithmetic and copies ran while one was open for 4% of the time, Pallas kernels for 0%

commit v1 on v0

v1 whole, which is shorter than its diff:
```python
import jax
import jax.numpy as jnp
from jax import lax
from jax.experimental import pallas as pl
from jax.experimental.pallas import tpu as pltpu
from jax.sharding import PartitionSpec as P

MESH = pl.DeviceIdType.MESH
F32, BF16 = jnp.float32, jnp.bfloat16
NT = (((1,), (1,)), ((), ()))

R = 24
RC = 2 * R
HALF = 4096
EXT = 128
WID = HALF + EXT
CUT = 2176
Q = 2048
W0 = Q + 128
ROWS = 16 * RC
NMSG = 128


def kernel(vir_ref, occ_ref, pid_ref, b_ref, gamma_ref, dens_ref,
           A, B, st, snd, ip, ir, amp, ampt, ampd,
           acc0, hold0, l0, d0, rl0, rd0, rm0,
           acc1, hold1, l1, d1, rl1, rd1, rm1,
           rz, rp, f0, f1, ssem, rsem, osem):
    row, col = lax.axis_index("row"), lax.axis_index("col")
    x, y, z, c = col // 4, row % 4, (col // 2) % 2 * 4 + row // 4, col % 2

    def dev(x, y, z, c):
        return (z % 4 * 4 + y, x * 4 + z // 4 * 2 + c)

    xs = [dev((x + 1) % 4, y, z, c), dev((x + 3) % 4, y, z, c)]
    ys = [dev(x, (y + 1) % 4, z, c), dev(x, (y + 3) % 4, z, c)]
    zs = [dev(x, y, (z + 2) % 8, c), dev(x, y, (z + 6) % 8, c)]
    far = dev(x, y, (z + 4) % 8, c)
    pair = dev(x, y, z + 1 - 2 * (z % 2), c)
    core = dev(x, y, z, 1 - c)
    peers = xs + ys + zs + [far, pair, core]

    barrier = pltpu.get_barrier_semaphore()
    for p in peers:
        pl.semaphore_signal(barrier, inc=1, device_id=p, device_id_type=MESH)

    count = [0]

    def msg(src, dst, to):
        i = count[0]
        count[0] += 1
        return pltpu.make_async_remote_copy(
            src_ref=src, dst_ref=dst, send_sem=ssem.at[i], recv_sem=rsem.at[i],
            device_id=to, device_id_type=MESH)

    sent = []

    def go(m, later=True):
        m.start()
        if later:
            sent.append(m)
        return m

    lane = lax.broadcasted_iota(jnp.int32, (R, EXT), 1)
    e = vir_ref[...]
    diag = lax.broadcasted_iota(jnp.int32, (R, R), 0) == lax.broadcasted_iota(jnp.int32, (R, R), 1)
    e_hi = jnp.sum(jnp.where(diag, (e >> 6).astype(F32), 0.0), axis=1, keepdims=True) * (64.0 / 1024.0)
    e_lo = jnp.sum(jnp.where(diag, (e & 63).astype(F32), 0.0), axis=1, keepdims=True) * (1.0 / 1024.0)
    occ = occ_ref[...]
    place = lax.broadcasted_iota(jnp.int32, occ.shape, 0) * occ.shape[1] + lax.broadcasted_iota(
        jnp.int32, occ.shape, 1)

    def level(k):
        picked = jnp.where(place == pid_ref[k], occ.astype(F32), 0.0)
        return jnp.sum(jnp.sum(picked, axis=1, keepdims=True), axis=0, keepdims=True)

    zero = jnp.zeros((R, EXT), F32)
    exts = [jnp.where(lane == 0, e_hi, jnp.where(lane == 1, e_lo, jnp.where(
        lane < 4, 1.0, jnp.where(lane < 6, -1.0, zero))))]
    for k in range(2):
        s = level(0) + level(1 + k)
        s_hi = jnp.floor(s * (1.0 / 64.0))
        s_lo = s - s_hi * 64.0
        exts.append(jnp.where(lane < 2, 1.0, jnp.where(lane == 2, e_hi, jnp.where(lane == 3, e_lo, jnp.where(
            lane == 4, s_hi * (64.0 / 1024.0), jnp.where(lane == 5, s_lo * (1.0 / 1024.0), zero))))))

    mine = pl.multiple_of(c * R, 8)
    theirs = pl.multiple_of((1 - c) * R, 8)

    @pl.loop(0, HALF // 512)
    def _(n):
        o = n * 512
        for m in range(3):
            st[m, pl.ds(mine, R), pl.ds(pl.multiple_of(o, 128), 512)] = b_ref[
                m, :, pl.ds(pl.multiple_of(c * HALF + o, 128), 512)].astype(F32)
            snd[m, :, pl.ds(pl.multiple_of(o, 128), 512)] = b_ref[
                m, :, pl.ds(pl.multiple_of((1 - c) * HALF + o, 128), 512)].astype(F32)

    for m in range(3):
        st[m, pl.ds(mine, R), HALF:] = exts[m]
        snd[m, :, HALF:] = exts[m]

    pl.semaphore_wait(barrier, len(peers))

    swap = go(msg(snd, st.at[:, pl.ds(mine, R)], core))
    swap.wait_recv()

    @pl.loop(0, 3)
    def _(n):
        o = pl.ds(pl.multiple_of(n * 1408, 128), 1408)
        A[0:RC, o] = st[0, :, o].astype(BF16)
        for k in range(2):
            B[k * RC:(k + 1) * RC, o] = st[1 + k, :, o].astype(BF16)

    H = [pl.ds(0, CUT), pl.ds(CUT, WID - CUT)]

    class Ring:
        def __init__(self, buf, at, n, to):
            rows = lambda s: pl.ds(at[s], n)
            self.own = [[msg(buf.at[rows(0), H[h]], buf.at[rows((3, 1)[d]), H[h]], to[d]) for h in range(2)]
                        for d in range(2)]
            self.fwd = [msg(buf.at[rows((3, 1)[d]), H[d]], buf.at[rows(2), H[d]], to[d]) for d in range(2)]

        def first(self):
            for d in range(2):
                go(self.own[d][d])

        def second(self):
            for d in range(2):
                go(self.own[d][1 - d])

        def forward(self):
            for d in range(2):
                self.own[d][d].wait_recv()
                go(self.fwd[d])

        def finish(self):
            for d in range(2):
                self.own[d][1 - d].wait_recv()
            for d in range(2):
                self.fwd[d].wait_recv()

    zr = Ring(A, [i * 4 * RC for i in range(4)], RC, zs)
    xr = [Ring(A, [(i * 4 + j) * RC for j in range(4)], RC, xs) for i in range(4)]
    yr = [Ring(B, [(b * 4 + j) * 2 * RC for j in range(4)], 2 * RC, ys) for b in range(2)]
    pr = [msg(B.at[pl.ds(0, 2 * RC), H[h]], B.at[pl.ds(8 * RC, 2 * RC), H[h]], pair) for h in range(2)]

    zr.first()
    xr[0].first()
    yr[0].first()
    zr.second()
    xr[0].second()
    yr[0].second()
    go(pr[0])
    go(pr[1])
    xr[0].forward()
    zr.forward()
    go(xr[3].own[0][0])
    go(xr[1].own[1][1])
    go(xr[3].own[1][0])
    go(xr[1].own[0][1])
    yr[0].forward()
    for d in range(2):
        zr.own[d][1 - d].wait_recv()
    go(xr[3].own[0][1])
    go(xr[1].own[1][0])
    go(xr[3].own[1][1])
    go(xr[1].own[0][0])
    for h in range(2):
        pr[h].wait_recv()
    yr[1].first()
    yr[1].second()
    xr[3].forward()
    xr[1].forward()
    for d in range(2):
        zr.fwd[d].wait_recv()
    xr[2].first()
    xr[2].second()
    xr[2].forward()
    yr[1].forward()
    for r in [xr[0], yr[0], xr[3], xr[1], xr[2], yr[1]]:
        r.finish()

    HR = ROWS // 2
    parts = []
    for h in range(2):
        rows = pl.ds(h * HR, HR)

        @pl.loop(0, ROWS // 256)
        def _(n):
            o = pl.ds(pl.multiple_of(n * 256, 256), 256)
            ip[rows, o] = lax.dot_general(A[rows, 0:HALF], B[o, 0:HALF], NT, preferred_element_type=F32)

        parts.append(go(msg(ip.at[rows], ir.at[rows], core)))

    spot = [[((x + j) % 4 * 2 + (z + 2 * i) % 8 // 4) * RC for j in range(4)] for i in range(4)]
    for h in range(2):
        rows = pl.ds(h * HR, HR)
        parts[h].wait_recv()

        @pl.loop(0, ROWS // 256)
        def _(n):
            o = pl.ds(pl.multiple_of(n * 256, 256), 256)
            den = lax.dot_general(A[rows, HALF:], B[o, HALF:], NT, preferred_element_type=F32)
            t = ((ip[rows, o] + ir[rows, o]) / (0.0 - den)).astype(BF16)
            amp[rows, o] = t
            ampt[o, rows] = t.astype(F32).T.astype(BF16)
            for q in range(8):
                i, j = h * 2 + q // 4, q % 4
                to = pl.multiple_of((i % 2) * HR + spot[i][j], 16)
                ampd[pl.ds(to, RC), o] = t[q * RC:(q + 1) * RC]

    def store(b, w, cs, out, h, n, acc, hold, l, d):
        acc[b, h, :, cs] = out[0:n]
        l[b, h, :, cs] = out[2 * n:3 * n].astype(BF16)
        if h == 0:
            hold[w, 0, :, cs] = out[n:2 * n]
            d[b, 1, :, cs] = out[3 * n:4 * n].astype(BF16)
        else:
            hold[w, 1, :, cs] = out[3 * n:4 * n]
            d[b, 0, :, cs] = out[n:2 * n].astype(BF16)

    def product0(i):
        for h in range(2):
            lhs = amp[i * 4 * RC:(i + 1) * 4 * RC, :]

            @pl.loop(0, Q // 512)
            def _(n):
                o = pl.multiple_of(n * 512, 512)
                out = jnp.dot(lhs, B[:, pl.ds(o + h * Q, 512)], preferred_element_type=F32)
                store(i, 0, pl.ds(o, 512), out, h, RC, acc0, hold0, l0, d0)

            rhs = ampd[pl.ds(pl.multiple_of((i % 2) * HR + h * 128 + c * 128, 128), 128), :]
            out = lax.dot_general(lhs, rhs, NT, preferred_element_type=F32)
            store(i, 0, pl.ds(Q, 128), out, h, RC, acc0, hold0, l0, d0)

    def product1(b):
        for h in range(2):
            @pl.loop(0, Q // 256)
            def _(n):
                o = pl.multiple_of(n * 256, 256)
                out = jnp.dot(ampt[b * HR:(b + 1) * HR, :], A[:, pl.ds(o + h * Q, 256)], preferred_element_type=F32)
                store(b, b, pl.ds(o, 256), out, h, 2 * RC, acc1, hold1, l1, d1)

    class Sum:
        def __init__(self, b, w, to, acc, hold, l, d, rl, rd, rm):
            self.b, self.w, self.acc, self.hold, self.l, self.rd, self.rl, self.rm = b, w, acc, hold, l, rd, rl, rm
            self.m1 = [msg(l.at[b, f], rl.at[b, f], to[f]) for f in range(2)]
            self.md = [msg(d.at[b, f], rd.at[b, f], to[f]) for f in range(2)]
            self.m2 = [msg(l.at[b, f], rm.at[b, f], to[f]) for f in range(2)]

        def start(self):
            for m in self.m1:
                go(m, False)
            for m in self.md:
                go(m, False)

        def relay(self):
            for f in range(2):
                self.m1[f].wait_send()
                self.m1[f].wait_recv()
                self.l[self.b, f] = (self.hold[self.w, f] + self.rl[self.b, f].astype(F32)).astype(BF16)
                go(self.m2[f])

        def finish(self):
            for f in range(2):
                self.md[f].wait_send()
                self.md[f].wait_recv()
            for f in range(2):
                self.m2[f].wait_recv()
                self.acc[self.b, f] = (self.acc[self.b, f] + self.rm[self.b, f].astype(F32)
                                       + self.rd[self.b, 1 - f].astype(F32))

    s0 = [Sum(i, 0, xs, acc0, hold0, l0, d0, rl0, rd0, rm0) for i in range(4)]
    s1 = [Sum(b, b, ys, acc1, hold1, l1, d1, rl1, rd1, rm1) for b in range(2)]
    mz = [None] + [msg(d0.at[i], rz.at[3 - i], (zs[0], far, zs[1])[i - 1]) for i in (1, 2, 3)]
    mp = msg(d1.at[1], rp, pair)

    def onward0(i):
        s0[i].finish()
        d0[i] = acc0[i].astype(BF16)
        go(mz[i])

    product0(2)
    s0[2].start()
    product1(1)
    s1[1].start()
    s0[2].relay()
    product0(1)
    s0[1].start()
    product1(0)
    s1[1].relay()
    s1[0].start()
    onward0(2)
    s0[1].relay()
    product0(3)
    s0[3].start()
    onward0(1)
    s1[1].finish()
    d1[1] = acc1[1].astype(BF16)
    go(mp)
    s0[3].relay()
    product0(0)
    s0[0].start()
    s1[0].relay()
    onward0(3)
    s0[0].relay()
    s0[0].finish()
    for i in (2, 1, 3):
        mz[i].wait_recv()
    for h in range(2):
        acc0[0, h] = acc0[0, h] + rz[0, h].astype(F32) + rz[1, h].astype(F32) + rz[2, h].astype(F32)
    x0 = go(msg(acc0.at[0, :, pl.ds(theirs, R)], f0, core))
    outs = []

    def put(src, dst):
        cp = pltpu.make_async_copy(src, dst, osem.at[len(outs)])
        cp.start()
        outs.append(cp)

    def cols(core_, h):
        return pl.ds(pl.multiple_of(core_ * HALF + h * Q, 128), Q)

    for h in range(2):
        put(acc0.at[0, h, pl.ds(mine, R), pl.ds(0, Q)], gamma_ref.at[0, :, cols(c, h)])
        put(acc0.at[0, h, pl.ds(mine, R), pl.ds(Q, 128)],
            dens_ref.at[:, pl.ds(pl.multiple_of((c + h) * 128, 128), 128)])
    mp.wait_recv()
    s1[0].finish()
    for h in range(2):
        acc1[0, h] = acc1[0, h] + rp[h].astype(F32)
    x1 = []
    for k in range(2):
        x1.append(go(msg(acc1.at[0, :, pl.ds(pl.multiple_of(k * RC + theirs, 8), R)], f1.at[k], core)))
        for h in range(2):
            put(acc1.at[0, h, pl.ds(pl.multiple_of(k * RC + mine, 8), R)], gamma_ref.at[1 + k, :, cols(c, h)])
    x0.wait_recv()
    for h in range(2):
        put(f0.at[h, :, pl.ds(0, Q)], gamma_ref.at[0, :, cols(1 - c, h)])
    put(f0.at[1 - c, :, pl.ds(Q, 128)], dens_ref.at[:, pl.ds(pl.multiple_of((1 - c) * 256, 128), 128)])
    for k in range(2):
        x1[k].wait_recv()
        for h in range(2):
            put(f1.at[k, h], gamma_ref.at[1 + k, :, cols(1 - c, h)])
    for m in sent:
        m.wait_send()
    for cp in outs:
        cp.wait()


def shards(b_factors, occ_energy, vir_energy, pair_ids):
    vm = pl.BlockSpec(memory_space=pltpu.VMEM)
    V = pltpu.VMEM
    return pl.pallas_call(
        kernel,
        out_shape=(jax.ShapeDtypeStruct((3, R, 2 * HALF), F32), jax.ShapeDtypeStruct((R, 16 * R), F32)),
        in_specs=[vm, vm, pl.BlockSpec(memory_space=pltpu.SMEM), vm],
        out_specs=(pl.BlockSpec(memory_space=pl.ANY), pl.BlockSpec(memory_space=pl.ANY)),
        scratch_shapes=[
            V((ROWS, WID), BF16), V((ROWS, WID), BF16), V((3, RC, WID), F32), V((3, R, WID), F32),
            V((ROWS, ROWS), F32), V((ROWS, ROWS), F32),
            V((ROWS, ROWS), BF16), V((ROWS, ROWS), BF16), V((ROWS, ROWS), BF16),
            V((4, 2, RC, W0), F32), V((1, 2, RC, W0), F32), V((4, 2, RC, W0), BF16), V((4, 2, RC, W0), BF16),
            V((4, 2, RC, W0), BF16), V((4, 2, RC, W0), BF16), V((4, 2, RC, W0), BF16),
            V((2, 2, 2 * RC, Q), F32), V((2, 2, 2 * RC, Q), F32), V((2, 2, 2 * RC, Q), BF16),
            V((2, 2, 2 * RC, Q), BF16),
            V((2, 2, 2 * RC, Q), BF16), V((2, 2, 2 * RC, Q), BF16), V((2, 2, 2 * RC, Q), BF16),
            V((3, 2, RC, W0), BF16), V((2, 2 * RC, Q), BF16),
            V((2, R, W0), F32), V((2, 2, R, Q), F32),
            pltpu.SemaphoreType.DMA((NMSG,)), pltpu.SemaphoreType.DMA((NMSG,)), pltpu.SemaphoreType.DMA((16,)),
        ],
        compiler_params=pltpu.CompilerParams(
            collective_id=0, has_side_effects=True, vmem_limit_bytes=61 * 2**20),
        cost_estimate=pl.CostEstimate(flops=15 * 10**9, bytes_accessed=4 * 10**6, transcendentals=0),
        name="mp2",
    )(vir_energy.reshape(1, R), occ_energy.reshape(12, 128), pair_ids, b_factors)


def solution(mesh):
    in_specs = (P(None, ("row", "col"), None), P(), P(("row", "col")), P())
    out_specs = (P(None, ("row", "col"), None), P(("row", "col"), None))
    return jax.shard_map(shards, mesh=mesh, in_specs=in_specs, out_specs=out_specs, check_vma=False)
```

time: 824 us -> 178 us (0.22)
  waiting for transfers between devices: 707 us -> 0 us
  Pallas kernels: 0 us -> 174 us
  matrix products: 54.5 us -> 0 us
  blocking collectives: 27.2 us -> 0 us
  between operations: 17.9 us -> 0.65 us
    reduce_scatter x3 -> x0, waiting for transfers between devices: 435 us -> none  [the longest x2 285 us: shards(): lax.psum_scatter(lax.dot_general(cols, a_panel, (((0,), (0,)), ((), ())),...]
    all_gather x2 -> x0, waiting for transfers between devices: 197 us -> none  [the longest x1 140 us: shards(): lax.all_gather(b_factors[1:], 'row', axis=1, tiled=True)]
    pallas_call x0 -> x1, Pallas kernels: none -> 174 us  [shards(): pl.pallas_call(kernel, out_shape=(jax.ShapeDtypeStruct((3, R, 2 * HALF),...]
    unnamed x7 -> x0, waiting for transfers between devices: 74.9 us -> none
    dot_general x8 -> x0, matrix products: 54.5 us -> none  [the longest x2 23.7 us: shards(): lax.dot_general(cols, a_panel, (((0,), (0,)), ((), ())), preferred_elemen...]
    unnamed x2 -> x0, blocking collectives: 27.2 us -> none
  transfers between devices with their start and end apart: 6 -> 0, of which waited for: 6 -> 0; matrix products, arithmetic and copies ran while one was open for 4% -> 0% of each run, Pallas kernels for 0% -> 0%
where the time goes in v1:
time: 178 us
  Pallas kernels  174 us (98%)
  local copies, waits for them, and re-layouts  3.85 us (2%)
    pallas_call x1, Pallas kernels, shards(): pl.pallas_call(kernel, out_shape=(jax.ShapeDtypeStruct((3, R, 2 * HALF),...  174 us
    unnamed x4, local copies, waits for them, and re-layouts  3.85 us

profile of v1, /device:TPU:33, one launch (start us, length us, event | category | flops | bytes accessed | tf_op | source)
XLA Modules:
  0.0 178.3 jit_solution(15084927603832753195)
XLA Ops:
  0.6 173.8 %mp2.1 = (f32[3,24,8192]{2,1,0:T(8,128)}, f32[24,384]{1,0:T(8,128)}) custom-call(s32[1,24]{1,0:T(1,128)} %bitcast.3, s32[12,128]{1,0:T(8,128)} %bitcast.2, s32[3]{0:T(128)} %pid_ref.1, bf16[3,24,8192]{2,1,0:T(8,128)(2,1)} %b_ref.1), custom_call_target="tpu_custom_call" | custom-call | flops 15000000512 | bytes 4000000 | tf_op jit(solution)/shard_map/mp2/pallas_call | solution.py:354
  174.4 0.0 copy-start
  174.4 3.2 %copy.8 = f32[3,24,8192]{2,1,0:T(8,128)} copy(f32[3,24,8192]{2,1,0:T(8,128)} %get-tuple-element.4) | data formatting | bytes 4718592
  177.7 0.0 copy-done
  177.7 0.6 copy.9
Async XLA Ops:
  174.4 3.2 %copy-start = (f32[24,384]{1,0:T(8,128)S(1)}, f32[24,384]{1,0:T(8,128)}, u32[]{:S(2)}) copy-start(f32[24,384]{1,0:T(8,128)} %get-tuple-element.5) | copy-start | bytes 110596

commit v2 on v1

v2 whole, which is shorter than its diff:
```python
import jax
import jax.numpy as jnp
from jax import lax
from jax.experimental import pallas as pl
from jax.experimental.pallas import tpu as pltpu
from jax.sharding import PartitionSpec as P

MESH = pl.DeviceIdType.MESH
F32, BF16 = jnp.float32, jnp.bfloat16
NT = (((1,), (1,)), ((), ()))

R = 24
RC = 2 * R
HALF = 4096
EXT = 128
WID = HALF + EXT
CUT = 2176
Q = 2048
W0 = Q // 2 + 128
ROWS = 16 * RC
NMSG = 224
Q1, Q2 = Q // 2, Q // 4
ORD = (0, 1, 3, 2)
POS = tuple(ORD.index(k) for k in range(4))
CHUNK = ((2, 2), (1, 3), (3, 1), (0, 0))


def kernel(vir_ref, occ_ref, pid_ref, b_ref, gamma_ref, dens_ref,
           A, B, st, snd, ip, ir, amp, ampt, ampd,
           acc0, hold0, l0, d0, rl0, rd0, rm0,
           acc1, hold1, l1, d1, rl1, rd1, rm1,
           rz, rp, f0, f1, ssem, rsem, osem):
    row, col = lax.axis_index("row"), lax.axis_index("col")
    x, y, z, c = col // 4, row % 4, (col // 2) % 2 * 4 + row // 4, col % 2

    def dev(x, y, z, c):
        return (z % 4 * 4 + y, x * 4 + z // 4 * 2 + c)

    xs = [dev((x + 1) % 4, y, z, c), dev((x + 3) % 4, y, z, c)]
    ys = [dev(x, (y + 1) % 4, z, c), dev(x, (y + 3) % 4, z, c)]
    zs = [dev(x, y, (z + 2) % 8, c), dev(x, y, (z + 6) % 8, c)]
    far = dev(x, y, (z + 4) % 8, c)
    pair = dev(x, y, z + 1 - 2 * (z % 2), c)
    core = dev(x, y, z, 1 - c)
    peers = xs + ys + zs + [far, pair, core]

    barrier = pltpu.get_barrier_semaphore()
    for p in peers:
        pl.semaphore_signal(barrier, inc=1, device_id=p, device_id_type=MESH)

    count = [0]

    def msg(src, dst, to):
        i = count[0]
        count[0] += 1
        return pltpu.make_async_remote_copy(
            src_ref=src, dst_ref=dst, send_sem=ssem.at[i], recv_sem=rsem.at[i],
            device_id=to, device_id_type=MESH)

    sent = []

    def go(m, later=True):
        m.start()
        if later:
            sent.append(m)
        return m

    lane = lax.broadcasted_iota(jnp.int32, (R, EXT), 1)
    e = vir_ref[...]
    diag = lax.broadcasted_iota(jnp.int32, (R, R), 0) == lax.broadcasted_iota(jnp.int32, (R, R), 1)
    e_hi = jnp.sum(jnp.where(diag, (e >> 6).astype(F32), 0.0), axis=1, keepdims=True) * (64.0 / 1024.0)
    e_lo = jnp.sum(jnp.where(diag, (e & 63).astype(F32), 0.0), axis=1, keepdims=True) * (1.0 / 1024.0)
    occ = occ_ref[...]
    place = lax.broadcasted_iota(jnp.int32, occ.shape, 0) * occ.shape[1] + lax.broadcasted_iota(
        jnp.int32, occ.shape, 1)

    def level(k):
        picked = jnp.where(place == pid_ref[k], occ.astype(F32), 0.0)
        return jnp.sum(jnp.sum(picked, axis=1, keepdims=True), axis=0, keepdims=True)

    zero = jnp.zeros((R, EXT), F32)
    exts = [jnp.where(lane == 0, e_hi, jnp.where(lane == 1, e_lo, jnp.where(
        lane < 4, 1.0, jnp.where(lane < 6, -1.0, zero))))]
    for k in range(2):
        s = level(0) + level(1 + k)
        s_hi = jnp.floor(s * (1.0 / 64.0))
        s_lo = s - s_hi * 64.0
        exts.append(jnp.where(lane < 2, 1.0, jnp.where(lane == 2, e_hi, jnp.where(lane == 3, e_lo, jnp.where(
            lane == 4, s_hi * (64.0 / 1024.0), jnp.where(lane == 5, s_lo * (1.0 / 1024.0), zero))))))

    mine = pl.multiple_of(c * R, 8)
    theirs = pl.multiple_of((1 - c) * R, 8)

    @pl.loop(0, HALF // 512)
    def _(n):
        o = n * 512
        for m in range(3):
            st[m, pl.ds(mine, R), pl.ds(pl.multiple_of(o, 128), 512)] = b_ref[
                m, :, pl.ds(pl.multiple_of(c * HALF + o, 128), 512)].astype(F32)
            snd[m, :, pl.ds(pl.multiple_of(o, 128), 512)] = b_ref[
                m, :, pl.ds(pl.multiple_of((1 - c) * HALF + o, 128), 512)].astype(F32)

    for m in range(3):
        st[m, pl.ds(mine, R), HALF:] = exts[m]
        snd[m, :, HALF:] = exts[m]

    pl.semaphore_wait(barrier, len(peers))

    swap = go(msg(snd, st.at[:, pl.ds(mine, R)], core))
    swap.wait_recv()

    @pl.loop(0, 3)
    def _(n):
        o = pl.ds(pl.multiple_of(n * 1408, 128), 1408)
        A[0:RC, o] = st[0, :, o].astype(BF16)
        for k in range(2):
            B[k * RC:(k + 1) * RC, o] = st[1 + k, :, o].astype(BF16)

    def arow(i, j):
        return (POS[i] * 4 + POS[j]) * RC

    def brow(b, j):
        return (b * 4 + POS[j]) * 2 * RC

    H = [pl.ds(0, CUT), pl.ds(CUT, WID - CUT)]
    H4 = [pl.ds(0, 1152), pl.ds(1152, 1024), pl.ds(2176, 1024), pl.ds(3200, 1024)]

    class Ring:
        def __init__(self, buf, at, n, to, cut):
            rows = lambda s: pl.ds(at[s], n)
            self.own = [[msg(buf.at[rows(0), cut[h]], buf.at[rows((3, 1)[d]), cut[h]], to[d]) for h in range(2)]
                        for d in range(2)]
            self.fwd = [msg(buf.at[rows((3, 1)[d]), cut[d]], buf.at[rows(2), cut[d]], to[d]) for d in range(2)]

        def first(self):
            for d in range(2):
                go(self.own[d][d])

        def second(self):
            for d in range(2):
                go(self.own[d][1 - d])

        def forward(self, ds=(0, 1)):
            for d in ds:
                self.own[d][d].wait_recv()
                go(self.fwd[d])

        def rest(self):
            for d in range(2):
                self.own[d][1 - d].wait_recv()

        def finish(self):
            for d in range(2):
                self.fwd[d].wait_recv()

    zown = [[msg(A.at[pl.ds(0, RC), H[h]], A.at[pl.ds(arow((3, 1)[d], 0), RC), H[h]], zs[d]) for h in range(2)]
            for d in range(2)]
    zfar = [[msg(A.at[pl.ds(arow((3, 1)[d], 0), RC), H4[2 * d + p]], A.at[pl.ds(arow(2, 0), RC), H4[2 * d + p]], zs[d])
             for p in range(2)] for d in range(2)]
    xr = [Ring(A, [arow(i, j) for j in range(4)], RC, xs, H) for i in (0, 1, 3)]
    x0, x1, x3 = xr
    x2 = [Ring(A, [arow(2, j) for j in range(4)], RC, xs, [H4[p], H4[2 + p]]) for p in range(2)]
    y0 = Ring(B, [brow(0, j) for j in range(4)], 2 * RC, ys, H)
    y1 = [Ring(B, [brow(1, j) for j in range(4)], 2 * RC, ys, [H4[p], H4[2 + p]]) for p in range(2)]
    pr = [[msg(B.at[pl.ds(0, 2 * RC), H4[p + q]], B.at[pl.ds(brow(1, 0), 2 * RC), H4[p + q]], pair) for q in (0, 2)]
          for p in range(2)]

    def integral(r, n, o0, o1, w):
        @pl.loop(0, (o1 - o0) // w)
        def _(k):
            o = pl.ds(pl.multiple_of(o0 + k * w, 128), w)
            ip[r:r + n, o] = lax.dot_general(A[r:r + n, 0:HALF], B[o, 0:HALF], NT, preferred_element_type=F32)

    def swapped(r, n, o0, o1):
        part = (pl.ds(r, n), pl.ds(o0, o1 - o0))
        return go(msg(ip.at[part], ir.at[part], core))

    def slot(s):
        i, j = ORD[s // 4], ORD[s % 4]
        return i % 2 * (ROWS // 2) + ((x + j) % 4 * 2 + (z + 2 * i) % 8 // 4) * RC

    def amplitude(r, n, o0, o1):
        @pl.loop(0, (o1 - o0) // 128)
        def _(k):
            o = pl.ds(pl.multiple_of(o0 + k * 128, 128), 128)
            rows = pl.ds(r, n)
            den = lax.dot_general(A[rows, HALF:], B[o, HALF:], NT, preferred_element_type=F32)
            t = ((ip[rows, o] + ir[rows, o]) / (0.0 - den)).astype(BF16)
            amp[rows, o] = t
            ampt[o, rows] = t.astype(F32).T.astype(BF16)
            for s in range(16):
                lo, hi = max(r, s * RC), min(r + n, s * RC + RC)
                if lo < hi:
                    ampd[pl.ds(pl.multiple_of(slot(s) + lo - s * RC, 16), hi - lo), o] = t[lo - r:hi - r]

    for d in range(2):
        go(zown[d][d])
    x0.first()
    y0.first()
    for d in range(2):
        go(zown[d][1 - d])
    x0.second()
    y0.second()
    x0.forward()
    for d in range(2):
        zown[d][d].wait_recv()
    for q in range(2):
        go(pr[0][q])
    go(x3.own[0][0])
    go(x1.own[1][1])
    go(x3.own[1][0])
    go(x1.own[0][1])
    y0.forward()
    for d in range(2):
        zown[d][1 - d].wait_recv()
    for q in range(2):
        go(pr[1][q])
    go(x3.own[0][1])
    go(x1.own[1][0])
    go(x3.own[1][1])
    go(x1.own[0][0])
    x3.forward((0,))
    x1.forward((1,))
    for q in range(2):
        pr[0][q].wait_recv()
    y1[0].first()
    y1[0].second()
    for d in range(2):
        go(zfar[d][0])
    for r in (x0, y0):
        r.rest()
        r.finish()
    integral(0, 192, 0, 384, 128)
    x3.forward((1,))
    x1.forward((0,))
    for q in range(2):
        pr[1][q].wait_recv()
    y1[1].first()
    y1[1].second()
    for d in range(2):
        go(zfar[d][1])
    for d in range(2):
        zfar[d][0].wait_recv()
    x2[0].first()
    x2[0].second()
    y1[0].forward()
    for d in range(2):
        zfar[d][1].wait_recv()
    x2[1].first()
    x2[1].second()
    x2[0].forward()
    for r in (x1, x3):
        r.rest()
        r.finish()
    integral(192, 320, 0, 384, 128)
    y1[1].forward()
    x2[1].forward()
    for r in y1:
        r.rest()
    integral(0, 512, 384, 640, 256)
    early = swapped(0, 512, 0, 640)
    early.wait_recv()
    amplitude(0, 512, 0, 640)
    for r in x2:
        r.rest()
    for r in x2 + y1:
        r.finish()
    integral(512, 256, 0, 640, 128)
    late = [swapped(512, 256, 0, 640)]
    integral(0, ROWS, 640, ROWS, 128)
    late.append(swapped(0, ROWS, 640, ROWS))
    late[0].wait_recv()
    amplitude(512, 256, 0, 640)
    late[1].wait_recv()
    amplitude(0, ROWS, 640, ROWS)

    def store(t, h, n, cs, out, acc, hold, l, d):
        acc[t, h, :, cs] = out[0:n]
        l[t, h, :, cs] = out[3 * n:4 * n].astype(BF16)
        if h == 0:
            hold[t % 2, 0, :, cs] = out[n:2 * n]
            d[t, 1, :, cs] = out[2 * n:3 * n].astype(BF16)
        else:
            hold[t % 2, 1, :, cs] = out[2 * n:3 * n]
            d[t, 0, :, cs] = out[n:2 * n].astype(BF16)

    def product0(t, h):
        i, s = CHUNK[t // 2][h], t % 2
        lhs = amp[POS[i] * 4 * RC:(POS[i] + 1) * 4 * RC, :]

        @pl.loop(0, Q1 // 512)
        def _(n):
            o = pl.multiple_of(n * 512, 512)
            out = jnp.dot(lhs, B[:, pl.ds(o + h * Q + s * Q1, 512)], preferred_element_type=F32)
            store(t, h, RC, pl.ds(o, 512), out, acc0, hold0, l0, d0)

        if s == 1:
            rhs = ampd[pl.ds(pl.multiple_of(i % 2 * (ROWS // 2) + h * 128 + c * 128, 128), 128), :]
            out = lax.dot_general(lhs, rhs, NT, preferred_element_type=F32)
            store(t, h, RC, pl.ds(Q1, 128), out, acc0, hold0, l0, d0)

    def product1(t, h):
        b, s = 1 - t // 4, t % 4
        lhs = ampt[b * ROWS // 2:(b + 1) * ROWS // 2, :]

        @pl.loop(0, Q2 // 256)
        def _(n):
            o = pl.multiple_of(n * 256, 256)
            out = jnp.dot(lhs, A[:, pl.ds(o + s * Q1 + h * Q2, 256)], preferred_element_type=F32)
            store(t, h, 2 * RC, pl.ds(o, 256), out, acc1, hold1, l1, d1)

    class Sum:
        def __init__(self, t, width, to, product, acc, hold, l, d, rl, rd, rm):
            w = pl.ds(0, width)
            full = pl.ds(0, acc.shape[2])
            self.t, self.w, self.product = t, w, product
            self.acc, self.hold, self.l, self.rd, self.rl, self.rm = acc, hold, l, rd, rl, rm
            self.m1 = [msg(l.at[t, f, full, w], rl.at[t, f, full, w], to[f]) for f in range(2)]
            self.md = [msg(d.at[t, f, full, w], rd.at[t, f, full, w], to[f]) for f in range(2)]
            self.m2 = [msg(l.at[t, f, full, w], rm.at[t, f, full, w], to[f]) for f in range(2)]

        def start(self):
            for f in range(2):
                self.product(self.t, f)
                go(self.m1[f], False)
            for f in (1, 0):
                go(self.md[f], False)

        def relay(self):
            t, w = self.t, self.w
            for f in range(2):
                self.m1[f].wait_send()
                self.m1[f].wait_recv()
                self.l[t, f, :, w] = (self.hold[t % 2, f, :, w] + self.rl[t, f, :, w].astype(F32)).astype(BF16)
                go(self.m2[f])

        def total(self, h):
            t, w = self.t, self.w
            return (self.acc[t, h, :, w] + self.rm[t, h, :, w].astype(F32) + self.rd[t, 1 - h, :, w].astype(F32))

        def finish(self):
            for f in range(2):
                self.md[f].wait_send()
                self.md[f].wait_recv()
            for f in range(2):
                self.m2[f].wait_recv()

    s0 = [Sum(t, Q1 + t % 2 * 128, xs, product0, acc0, hold0, l0, d0, rl0, rd0, rm0) for t in range(8)]
    s1 = [Sum(t, Q2, ys, product1, acc1, hold1, l1, d1, rl1, rd1, rm1) for t in range(8)]

    def zmsgs(t, k, flip):
        w = (pl.ds(0, RC), s0[t].w)
        return [msg(d0.at[(t, 1 - f if flip else f) + w], rz.at[(k, t % 2, f) + w], zs[f]) for f in range(2)]

    zl = [zmsgs(t, 0, False) for t in (0, 1)]
    zm = [zmsgs(t, 1, False) for t in (2, 3)]
    zd = [zmsgs(t, 2, True) for t in (4, 5)]
    mp = [msg(d1.at[t], rp.at[t], pair) for t in range(4)]
    outs = []

    def put(src, dst):
        cp = pltpu.make_async_copy(src, dst, osem.at[len(outs)])
        cp.start()
        outs.append(cp)

    def cols(core_, o, n):
        return pl.ds(pl.multiple_of(core_ * HALF + o, 128), n)

    f0m, f1m = [], []

    def done0(t):
        s0[t].finish()
        p, s, w = t // 2, t % 2, s0[t].w
        for f in range(2):
            if p == 0:
                d0[t, f, :, w] = s0[t].total(f).astype(BF16)
                go(zl[s][f])
            elif p == 1:
                zl[s][f].wait_recv()
                d0[t, f, :, w] = (s0[t].total(f) + rz[0, s, f, :, w].astype(F32)).astype(BF16)
                go(zm[s][f])
            elif p == 2:
                d0[t, 1 - f, :, w] = s0[t].total(1 - f).astype(BF16)
                go(zd[s][f])
            else:
                zm[s][f].wait_recv()
                zd[s][f].wait_recv()
        if p == 3:
            for h in range(2):
                acc0[t, h, :, w] = (s0[t].total(h) + rz[1, s, h, :, w].astype(F32)
                                    + rz[2, s, 1 - h, :, w].astype(F32))
            f0m.append(go(msg(acc0.at[t, :, pl.ds(theirs, R), w], f0.at[s, :, :, w], core)))
            for h in range(2):
                put(acc0.at[t, h, pl.ds(mine, R), pl.ds(0, Q1)], gamma_ref.at[0, :, cols(c, h * Q + s * Q1, Q1)])
                if s == 1:
                    put(acc0.at[t, h, pl.ds(mine, R), pl.ds(Q1, 128)],
                        dens_ref.at[:, pl.ds(pl.multiple_of((c + h) * 128, 128), 128)])

    def land0(s):
        f0m[s].wait_recv()
        for h in range(2):
            put(f0.at[s, h, :, pl.ds(0, Q1)], gamma_ref.at[0, :, cols(1 - c, h * Q + s * Q1, Q1)])
        if s == 1:
            put(f0.at[s, 1 - c, :, pl.ds(Q1, 128)],
                dens_ref.at[:, pl.ds(pl.multiple_of((1 - c) * 256, 128), 128)])

    def done1(t):
        s1[t].finish()
        if t < 4:
            for h in range(2):
                d1[t, h] = s1[t].total(h).astype(BF16)
            go(mp[t])
            return
        s = t - 4
        mp[s].wait_recv()
        for h in range(2):
            acc1[t, h] = s1[t].total(h) + rp[s, h].astype(F32)
        for k in range(2):
            f1m.append(go(msg(acc1.at[t, :, pl.ds(pl.multiple_of(k * RC + theirs, 8), R)], f1.at[s, k], core)))
        for k in range(2):
            for h in range(2):
                put(acc1.at[t, h, pl.ds(pl.multiple_of(k * RC + mine, 8), R)],
                    gamma_ref.at[1 + k, :, cols(c, s * Q1 + h * Q2, Q2)])

    def land1(s):
        for k in range(2):
            f1m[s * 2 + k].wait_recv()
            for h in range(2):
                put(f1.at[s, k, h], gamma_ref.at[1 + k, :, cols(1 - c, s * Q1 + h * Q2, Q2)])

    s0[0].start()
    s1[0].start()
    s0[0].relay()
    s0[1].start()
    s1[0].relay()
    s1[1].start()
    done0(0)
    done1(0)
    for t in range(1, 8):
        if t < 7:
            s0[t + 1].start()
            s1[t + 1].start()
        s0[t].relay()
        s1[t].relay()
        if t > 1:
            done0(t - 1)
            done1(t - 1)
        if t - 2 >= 4:
            land1(t - 6)
    land0(0)
    land1(2)
    done0(7)
    done1(7)
    land0(1)
    land1(3)
    for m in sent:
        m.wait_send()
    for cp in outs:
        cp.wait()


def shards(b_factors, occ_energy, vir_energy, pair_ids):
    vm = pl.BlockSpec(memory_space=pltpu.VMEM)
    V = pltpu.VMEM
    return pl.pallas_call(
        kernel,
        out_shape=(jax.ShapeDtypeStruct((3, R, 2 * HALF), F32), jax.ShapeDtypeStruct((R, 16 * R), F32)),
        in_specs=[vm, vm, pl.BlockSpec(memory_space=pltpu.SMEM), vm],
        out_specs=(pl.BlockSpec(memory_space=pl.ANY), pl.BlockSpec(memory_space=pl.ANY)),
        scratch_shapes=[
            V((ROWS, WID), BF16), V((ROWS, WID), BF16), V((3, RC, WID), F32), V((3, R, WID), F32),
            V((ROWS, ROWS), F32), V((ROWS, ROWS), F32),
            V((ROWS, ROWS), BF16), V((ROWS, ROWS), BF16), V((ROWS, ROWS), BF16),
            V((8, 2, RC, W0), F32), V((2, 2, RC, W0), F32), V((8, 2, RC, W0), BF16), V((8, 2, RC, W0), BF16),
            V((8, 2, RC, W0), BF16), V((8, 2, RC, W0), BF16), V((8, 2, RC, W0), BF16),
            V((8, 2, 2 * RC, Q2), F32), V((2, 2, 2 * RC, Q2), F32), V((8, 2, 2 * RC, Q2), BF16),
            V((8, 2, 2 * RC, Q2), BF16),
            V((8, 2, 2 * RC, Q2), BF16), V((8, 2, 2 * RC, Q2), BF16), V((8, 2, 2 * RC, Q2), BF16),
            V((3, 2, 2, RC, W0), BF16), V((4, 2, 2 * RC, Q2), BF16),
            V((2, 2, R, W0), F32), V((4, 2, 2, R, Q2), F32),
            pltpu.SemaphoreType.DMA((NMSG,)), pltpu.SemaphoreType.DMA((NMSG,)), pltpu.SemaphoreType.DMA((64,)),
        ],
        compiler_params=pltpu.CompilerParams(
            collective_id=0, has_side_effects=True, vmem_limit_bytes=61 * 2**20),
        cost_estimate=pl.CostEstimate(flops=15 * 10**9, bytes_accessed=4 * 10**6, transcendentals=0),
        name="mp2",
    )(vir_energy.reshape(1, R), occ_energy.reshape(12, 128), pair_ids, b_factors)


def solution(mesh):
    in_specs = (P(None, ("row", "col"), None), P(), P(("row", "col")), P())
    out_specs = (P(None, ("row", "col"), None), P(("row", "col"), None))
    return jax.shard_map(shards, mesh=mesh, in_specs=in_specs, out_specs=out_specs, check_vma=False)
```

time: 178 us -> 151 us (0.85); the launches traced: 178 us -> 149 us
  Pallas kernels: 174 us -> 144 us
    pallas_call x1, Pallas kernels: 174 us -> 144 us  [shards(): pl.pallas_call(kernel, out_shape=(jax.ShapeDtypeStruct((3, R, 2 * HALF),...]
where the time goes in v2:
time: 151 us; the launch traced here: 149 us
  Pallas kernels  144 us (95%)
  local copies, waits for them, and re-layouts  3.85 us (3%)
    pallas_call x1, Pallas kernels, shards(): pl.pallas_call(kernel, out_shape=(jax.ShapeDtypeStruct((3, R, 2 * HALF),...  144 us
    unnamed x4, local copies, waits for them, and re-layouts  3.85 us

profile of v2, /device:TPU:33, one launch (start us, length us, event | category | flops | bytes accessed | tf_op | source)
XLA Modules:
  0.0 148.7 jit_solution(16353515032490062569)
XLA Ops:
  0.6 144.2 %mp2.1 = (f32[3,24,8192]{2,1,0:T(8,128)}, f32[24,384]{1,0:T(8,128)}) custom-call(s32[1,24]{1,0:T(1,128)} %bitcast.3, s32[12,128]{1,0:T(8,128)} %bitcast.2, s32[3]{0:T(128)} %pid_ref.1, bf16[3,24,8192]{2,1,0:T(8,128)(2,1)} %b_ref.1), custom_call_target="tpu_custom_call" | custom-call | flops 15000000512 | bytes 4000000 | tf_op jit(solution)/shard_map/mp2/pallas_call | solution.py:465
  144.8 0.0 copy-start
  144.9 3.2 %copy.8 = f32[3,24,8192]{2,1,0:T(8,128)} copy(f32[3,24,8192]{2,1,0:T(8,128)} %get-tuple-element.4) | data formatting | bytes 4718592
  148.1 0.0 copy-done
  148.1 0.6 copy.9
Async XLA Ops:
  144.8 3.2 %copy-start = (f32[24,384]{1,0:T(8,128)S(1)}, f32[24,384]{1,0:T(8,128)}, u32[]{:S(2)}) copy-start(f32[24,384]{1,0:T(8,128)} %get-tuple-element.5) | copy-start | bytes 110596

commit v3 on v2

--- a/solution.py
+++ b/solution.py
@@ -14,7 +14,7 @@
 HALF = 4096
 EXT = 128
 WID = HALF + EXT
-CUT = 2176
+CUT = 2048
 Q = 2048
 W0 = Q // 2 + 128
 ROWS = 16 * RC
@@ -25,8 +25,8 @@
 CHUNK = ((2, 2), (1, 3), (3, 1), (0, 0))
 
 
-def kernel(vir_ref, occ_ref, pid_ref, b_ref, gamma_ref, dens_ref,
-           A, B, st, snd, ip, ir, amp, ampt, ampd,
+def kernel(vir_ref, occ_ref, pid_ref, b_hbm, gamma_ref, dens_ref,
+           b_ref, A, B, st, snd, ip, ir, amp, ampt, ampd,
            acc0, hold0, l0, d0, rl0, rd0, rm0,
            acc1, hold1, l1, d1, rl1, rd1, rm1,
            rz, rp, f0, f1, ssem, rsem, osem):
@@ -47,6 +47,9 @@
     barrier = pltpu.get_barrier_semaphore()
     for p in peers:
         pl.semaphore_signal(barrier, inc=1, device_id=p, device_id_type=MESH)
+
+    load = pltpu.make_async_copy(b_hbm, b_ref, osem.at[63])
+    load.start()
 
     count = [0]
 
@@ -91,30 +94,22 @@
     mine = pl.multiple_of(c * R, 8)
     theirs = pl.multiple_of((1 - c) * R, 8)
 
-    @pl.loop(0, HALF // 512)
-    def _(n):
-        o = n * 512
-        for m in range(3):
-            st[m, pl.ds(mine, R), pl.ds(pl.multiple_of(o, 128), 512)] = b_ref[
-                m, :, pl.ds(pl.multiple_of(c * HALF + o, 128), 512)].astype(F32)
-            snd[m, :, pl.ds(pl.multiple_of(o, 128), 512)] = b_ref[
-                m, :, pl.ds(pl.multiple_of((1 - c) * HALF + o, 128), 512)].astype(F32)
+    load.wait()
+
+    @pl.loop(0, 3)
+    def _(m):
+        @pl.loop(0, HALF // 512)
+        def _(n):
+            o = pl.multiple_of(n * 512, 128)
+            st[m, pl.ds(mine, R), pl.ds(o, 512)] = b_ref[m, :, pl.ds(pl.multiple_of(c * HALF + o, 128), 512)].astype(F32)
+            snd[m, :, pl.ds(o, 512)] = b_ref[m, :, pl.ds(pl.multiple_of((1 - c) * HALF + o, 128), 512)].astype(F32)
 
     for m in range(3):
         st[m, pl.ds(mine, R), HALF:] = exts[m]
         snd[m, :, HALF:] = exts[m]
 
     pl.semaphore_wait(barrier, len(peers))
-
-    swap = go(msg(snd, st.at[:, pl.ds(mine, R)], core))
-    swap.wait_recv()
-
-    @pl.loop(0, 3)
-    def _(n):
-        o = pl.ds(pl.multiple_of(n * 1408, 128), 1408)
-        A[0:RC, o] = st[0, :, o].astype(BF16)
-        for k in range(2):
-            B[k * RC:(k + 1) * RC, o] = st[1 + k, :, o].astype(BF16)
+    swap = [go(msg(snd.at[m], st.at[m, pl.ds(mine, R)], core)) for m in range(3)]
 
     def arow(i, j):
         return (POS[i] * 4 + POS[j]) * RC
@@ -123,7 +118,7 @@
         return (b * 4 + POS[j]) * 2 * RC
 
     H = [pl.ds(0, CUT), pl.ds(CUT, WID - CUT)]
-    H4 = [pl.ds(0, 1152), pl.ds(1152, 1024), pl.ds(2176, 1024), pl.ds(3200, 1024)]
+    H4 = [pl.ds(0, 1024), pl.ds(1024, 1024), pl.ds(2048, 1024), pl.ds(3072, WID - 3072)]
 
     class Ring:
         def __init__(self, buf, at, n, to, cut):
@@ -193,13 +188,24 @@
                 if lo < hi:
                     ampd[pl.ds(pl.multiple_of(slot(s) + lo - s * RC, 16), hi - lo), o] = t[lo - r:hi - r]
 
+    def settle(buf, to, m):
+        swap[m].wait_recv()
+
+        @pl.loop(0, 3)
+        def _(n):
+            o = pl.ds(pl.multiple_of(n * 1408, 128), 1408)
+            buf[to:to + RC, o] = st[m, :, o].astype(BF16)
+
+    settle(A, 0, 0)
     for d in range(2):
         go(zown[d][d])
     x0.first()
-    y0.first()
     for d in range(2):
         go(zown[d][1 - d])
     x0.second()
+    for k in range(2):
+        settle(B, k * RC, 1 + k)
+    y0.first()
     y0.second()
     x0.forward()
     for d in range(2):
@@ -259,13 +265,16 @@
         r.rest()
     integral(0, 512, 384, 640, 256)
     early = swapped(0, 512, 0, 640)
+    x2[0].rest()
+    x2[0].finish()
+    y1[0].finish()
     early.wait_recv()
     amplitude(0, 512, 0, 640)
-    for r in x2:
-        r.rest()
-    for r in x2 + y1:
-        r.finish()
-    integral(512, 256, 0, 640, 128)
+    x2[1].rest()
+    x2[1].finish()
+    y1[1].finish()
+    integral(512, 256, 0, 512, 256)
+    integral(512, 256, 512, 640, 128)
     late = [swapped(512, 256, 0, 640)]
     integral(0, ROWS, 640, ROWS, 128)
     late.append(swapped(0, ROWS, 640, ROWS))
@@ -319,12 +328,18 @@
             self.md = [msg(d.at[t, f, full, w], rd.at[t, f, full, w], to[f]) for f in range(2)]
             self.m2 = [msg(l.at[t, f, full, w], rm.at[t, f, full, w], to[f]) for f in range(2)]
 
-        def start(self):
+        def lead(self):
             for f in range(2):
                 self.product(self.t, f)
                 go(self.m1[f], False)
+
+        def follow(self):
             for f in (1, 0):
                 go(self.md[f], False)
+
+        def start(self):
+            self.lead()
+            self.follow()
 
         def relay(self):
             t, w = self.t, self.w
@@ -438,10 +453,13 @@
     done1(0)
     for t in range(1, 8):
         if t < 7:
-            s0[t + 1].start()
-            s1[t + 1].start()
+            s0[t + 1].lead()
+            s1[t + 1].lead()
         s0[t].relay()
         s1[t].relay()
+        if t < 7:
+            s0[t + 1].follow()
+            s1[t + 1].follow()
         if t > 1:
             done0(t - 1)
             done1(t - 1)
@@ -459,16 +477,32 @@
         cp.wait()
 
 
+def write(gamma_in, dens_in, gamma_ref, dens_ref, gamma_via, dens_via, sem):
+    parts = [(gamma_in.at[k, pl.ds(8 * r, 8)], gamma_via.at[k, pl.ds(8 * r, 8)], gamma_ref.at[k, pl.ds(8 * r, 8)])
+             for k in range(3) for r in range(3)] + [(dens_in, dens_via, dens_ref)]
+    come = [pltpu.make_async_copy(p[0], p[1], sem.at[0, n]) for n, p in enumerate(parts)]
+    leave = [pltpu.make_async_copy(p[1], p[2], sem.at[1, n]) for n, p in enumerate(parts)]
+    for cp in come:
+        cp.start()
+    for cp, then in zip(come, leave):
+        cp.wait()
+        then.start()
+    for cp in leave:
+        cp.wait()
+
+
 def shards(b_factors, occ_energy, vir_energy, pair_ids):
     vm = pl.BlockSpec(memory_space=pltpu.VMEM)
     V = pltpu.VMEM
-    return pl.pallas_call(
+    shapes = (jax.ShapeDtypeStruct((3, R, 2 * HALF), F32), jax.ShapeDtypeStruct((R, 16 * R), F32))
+    anywhere = pl.BlockSpec(memory_space=pl.ANY)
+    gamma, density = pl.pallas_call(
         kernel,
-        out_shape=(jax.ShapeDtypeStruct((3, R, 2 * HALF), F32), jax.ShapeDtypeStruct((R, 16 * R), F32)),
-        in_specs=[vm, vm, pl.BlockSpec(memory_space=pltpu.SMEM), vm],
-        out_specs=(pl.BlockSpec(memory_space=pl.ANY), pl.BlockSpec(memory_space=pl.ANY)),
+        out_shape=shapes,
+        in_specs=[vm, vm, pl.BlockSpec(memory_space=pltpu.SMEM), anywhere],
+        out_specs=(anywhere, anywhere),
         scratch_shapes=[
-            V((ROWS, WID), BF16), V((ROWS, WID), BF16), V((3, RC, WID), F32), V((3, R, WID), F32),
+            V((3, R, 2 * HALF), BF16), V((ROWS, WID), BF16), V((ROWS, WID), BF16), V((3, RC, WID), F32), V((3, R, WID), F32),
             V((ROWS, ROWS), F32), V((ROWS, ROWS), F32),
             V((ROWS, ROWS), BF16), V((ROWS, ROWS), BF16), V((ROWS, ROWS), BF16),
             V((8, 2, RC, W0), F32), V((2, 2, RC, W0), F32), V((8, 2, RC, W0), BF16), V((8, 2, RC, W0), BF16),
@@ -485,6 +519,10 @@
         cost_estimate=pl.CostEstimate(flops=15 * 10**9, bytes_accessed=4 * 10**6, transcendentals=0),
         name="mp2",
     )(vir_energy.reshape(1, R), occ_energy.reshape(12, 128), pair_ids, b_factors)
+    return pl.pallas_call(
+        write, out_shape=shapes, in_specs=[anywhere, anywhere], out_specs=(anywhere, anywhere),
+        scratch_shapes=[V((3, R, 2 * HALF), F32), V((R, 16 * R), F32), pltpu.SemaphoreType.DMA((2, 10))], name="write",
+    )(gamma, density)
 
 
 def solution(mesh):

time: 151 us -> 147 us (0.974)
  local copies, waits for them, and re-layouts: 3.85 us -> 0 us
    unnamed x4 -> x0, local copies, waits for them, and re-layouts: 3.85 us -> none
    pallas_call x1 -> x2, Pallas kernels: 144 us -> 144 us  [the longest x1 141 us: shards(): pl.pallas_call(kernel, out_shape=shapes, in_specs=[vm, vm, pl.BlockSpec(m...]
where the time goes in v3:
time: 147 us; the launch traced here: 145 us
  Pallas kernels  144 us (98%)
    pallas_call x1, Pallas kernels, shards(): pl.pallas_call(kernel, out_shape=shapes, in_specs=[vm, vm, pl.BlockSpec(m...  141 us

profile of v3, /device:TPU:33, one launch (start us, length us, event | category | flops | bytes accessed | tf_op | source)
XLA Modules:
  0.0 144.7 jit_solution(3602225191237641148)
XLA Ops:
  0.6 141.3 %mp2.1 = (f32[3,24,8192]{2,1,0:T(8,128)}, f32[24,384]{1,0:T(8,128)}) custom-call(s32[1,24]{1,0:T(1,128)} %bitcast.3, s32[12,128]{1,0:T(8,128)} %bitcast.2, s32[3]{0:T(128)} %pid_ref.1, bf16[3,24,8192]{2,1,0:T(8,128)(2,1)} %b_hbm.1), custom_call_target="tpu_custom_call" | custom-call | flops 15000000512 | bytes 4000000 | tf_op jit(solution)/shard_map/mp2/pallas_call | solution.py:499
  142.0 2.5 %write.1 = (f32[3,24,8192]{2,1,0:T(8,128)}, f32[24,384]{1,0:T(8,128)}) custom-call(f32[3,24,8192]{2,1,0:T(8,128)} %get-tuple-element.4.gamma_in, f32[24,384]{1,0:T(8,128)} %get-tuple-element.5.dens_in), custom_call_target="tpu_custom_call" | custom-call | tf_op jit(solution)/shard_map/write/pallas_call | solution.py:522

commit v4 on v3

--- a/solution.py
+++ b/solution.py
@@ -29,6 +29,7 @@
            b_ref, A, B, st, snd, ip, ir, amp, ampt, ampd,
            acc0, hold0, l0, d0, rl0, rd0, rm0,
            acc1, hold1, l1, d1, rl1, rd1, rm1,
+           acc2, hold2, l2, d2, rl2, rd2, rm2,
            rz, rp, f0, f1, ssem, rsem, osem):
     row, col = lax.axis_index("row"), lax.axis_index("col")
     x, y, z, c = col // 4, row % 4, (col // 2) % 2 * 4 + row // 4, col % 2
@@ -303,10 +304,8 @@
             out = jnp.dot(lhs, B[:, pl.ds(o + h * Q + s * Q1, 512)], preferred_element_type=F32)
             store(t, h, RC, pl.ds(o, 512), out, acc0, hold0, l0, d0)
 
-        if s == 1:
-            rhs = ampd[pl.ds(pl.multiple_of(i % 2 * (ROWS // 2) + h * 128 + c * 128, 128), 128), :]
-            out = lax.dot_general(lhs, rhs, NT, preferred_element_type=F32)
-            store(t, h, RC, pl.ds(Q1, 128), out, acc0, hold0, l0, d0)
+        if t == 7:
+            store(t, h, RC, pl.ds(Q1, 128), s2.total(h), acc0, hold0, l0, d0)
 
     def product1(t, h):
         b, s = 1 - t // 4, t % 4
@@ -317,6 +316,20 @@
             o = pl.multiple_of(n * 256, 256)
             out = jnp.dot(lhs, A[:, pl.ds(o + s * Q1 + h * Q2, 256)], preferred_element_type=F32)
             store(t, h, 2 * RC, pl.ds(o, 256), out, acc1, hold1, l1, d1)
+
+    def product2(t, h):
+        n = 4 * RC
+        for i in range(4):
+            rhs = ampd[pl.ds(pl.multiple_of(i % 2 * (ROWS // 2) + h * 128 + c * 128, 128), 128), :]
+            out = lax.dot_general(amp[POS[i] * n:(POS[i] + 1) * n, :], rhs, NT, preferred_element_type=F32)
+            if i == 0:
+                acc2[t, h] = out
+            elif i == 2:
+                l2[t, h] = out.astype(BF16)
+            elif i == 1 + 2 * h:
+                hold2[t, h] = out
+            else:
+                d2[t, 1 - h] = out.astype(BF16)
 
     class Sum:
         def __init__(self, t, width, to, product, acc, hold, l, d, rl, rd, rm):
@@ -360,7 +373,8 @@
             for f in range(2):
                 self.m2[f].wait_recv()
 
-    s0 = [Sum(t, Q1 + t % 2 * 128, xs, product0, acc0, hold0, l0, d0, rl0, rd0, rm0) for t in range(8)]
+    s2 = Sum(0, 128, zs, product2, acc2, hold2, l2, d2, rl2, rd2, rm2)
+    s0 = [Sum(t, Q1 + t // 7 * 128, xs, product0, acc0, hold0, l0, d0, rl0, rd0, rm0) for t in range(8)]
     s1 = [Sum(t, Q2, ys, product1, acc1, hold1, l1, d1, rl1, rd1, rm1) for t in range(8)]
 
     def zmsgs(t, k, flip):
@@ -402,8 +416,8 @@
                 zd[s][f].wait_recv()
         if p == 3:
             for h in range(2):
-                acc0[t, h, :, w] = (s0[t].total(h) + rz[1, s, h, :, w].astype(F32)
-                                    + rz[2, s, 1 - h, :, w].astype(F32))
+                acc0[t, h, :, w] = s0[t].total(h)
+                acc0[t, h, :, 0:Q1] += rz[1, s, h].astype(F32) + rz[2, s, 1 - h].astype(F32)
             f0m.append(go(msg(acc0.at[t, :, pl.ds(theirs, R), w], f0.at[s, :, :, w], core)))
             for h in range(2):
                 put(acc0.at[t, h, pl.ds(mine, R), pl.ds(0, Q1)], gamma_ref.at[0, :, cols(c, h * Q + s * Q1, Q1)])
@@ -445,9 +459,11 @@
 
     s0[0].start()
     s1[0].start()
+    s2.start()
     s0[0].relay()
     s0[1].start()
     s1[0].relay()
+    s2.relay()
     s1[1].start()
     done0(0)
     done1(0)
@@ -465,6 +481,8 @@
             done1(t - 1)
         if t - 2 >= 4:
             land1(t - 6)
+        if t == 3:
+            s2.finish()
     land0(0)
     land1(2)
     done0(7)
@@ -510,7 +528,10 @@
             V((8, 2, 2 * RC, Q2), F32), V((2, 2, 2 * RC, Q2), F32), V((8, 2, 2 * RC, Q2), BF16),
             V((8, 2, 2 * RC, Q2), BF16),
             V((8, 2, 2 * RC, Q2), BF16), V((8, 2, 2 * RC, Q2), BF16), V((8, 2, 2 * RC, Q2), BF16),
-            V((3, 2, 2, RC, W0), BF16), V((4, 2, 2 * RC, Q2), BF16),
+            V((1, 2, 4 * RC, 128), F32), V((1, 2, 4 * RC, 128), F32), V((1, 2, 4 * RC, 128), BF16),
+            V((1, 2, 4 * RC, 128), BF16),
+            V((1, 2, 4 * RC, 128), BF16), V((1, 2, 4 * RC, 128), BF16), V((1, 2, 4 * RC, 128), BF16),
+            V((3, 2, 2, RC, Q1), BF16), V((4, 2, 2 * RC, Q2), BF16),
             V((2, 2, R, W0), F32), V((4, 2, 2, R, Q2), F32),
             pltpu.SemaphoreType.DMA((NMSG,)), pltpu.SemaphoreType.DMA((NMSG,)), pltpu.SemaphoreType.DMA((64,)),
         ],

time: 147 us -> 145 us (0.986)
  Pallas kernels: 144 us -> 142 us
    pallas_call x1, Pallas kernels: 141 us -> 139 us  [shards(): pl.pallas_call(kernel, out_shape=shapes, in_specs=[vm, vm, pl.BlockSpec(m...]
where the time goes in v4:
time: 145 us; the launch traced here: 142 us
  Pallas kernels  142 us (98%)
    pallas_call x1, Pallas kernels, shards(): pl.pallas_call(kernel, out_shape=shapes, in_specs=[vm, vm, pl.BlockSpec(m...  139 us

profile of v4, /device:TPU:33, one launch (start us, length us, event | category | flops | bytes accessed | tf_op | source)
XLA Modules:
  0.0 142.3 jit_solution(8772092483595807528)
XLA Ops:
  0.6 139.0 %mp2.1 = (f32[3,24,8192]{2,1,0:T(8,128)}, f32[24,384]{1,0:T(8,128)}) custom-call(s32[1,24]{1,0:T(1,128)} %bitcast.3, s32[12,128]{1,0:T(8,128)} %bitcast.2, s32[3]{0:T(128)} %pid_ref.1, bf16[3,24,8192]{2,1,0:T(8,128)(2,1)} %b_hbm.1), custom_call_target="tpu_custom_call" | custom-call | flops 15000000512 | bytes 4000000 | tf_op jit(solution)/shard_map/mp2/pallas_call | solution.py:517
  139.7 2.5 %write.1 = (f32[3,24,8192]{2,1,0:T(8,128)}, f32[24,384]{1,0:T(8,128)}) custom-call(f32[3,24,8192]{2,1,0:T(8,128)} %get-tuple-element.4.gamma_in, f32[24,384]{1,0:T(8,128)} %get-tuple-element.5.dens_in), custom_call_target="tpu_custom_call" | custom-call | tf_op jit(solution)/shard_map/write/pallas_call | solution.py:543

commit v5 on v4

--- a/solution.py
+++ b/solution.py
@@ -206,13 +206,15 @@
     x0.second()
     for k in range(2):
         settle(B, k * RC, 1 + k)
+    for q in range(2):
+        go(pr[0][q])
     y0.first()
     y0.second()
     x0.forward()
     for d in range(2):
         zown[d][d].wait_recv()
     for q in range(2):
-        go(pr[0][q])
+        go(pr[1][q])
     go(x3.own[0][0])
     go(x1.own[1][1])
     go(x3.own[1][0])
@@ -220,8 +222,6 @@
     y0.forward()
     for d in range(2):
         zown[d][1 - d].wait_recv()
-    for q in range(2):
-        go(pr[1][q])
     go(x3.own[0][1])
     go(x1.own[1][0])
     go(x3.own[1][1])
@@ -237,7 +237,8 @@
     for r in (x0, y0):
         r.rest()
         r.finish()
-    integral(0, 192, 0, 384, 128)
+    integral(0, 192, 0, 256, 256)
+    integral(0, 192, 256, 384, 128)
     x3.forward((1,))
     x1.forward((0,))
     for q in range(2):
@@ -259,7 +260,8 @@
     for r in (x1, x3):
         r.rest()
         r.finish()
-    integral(192, 320, 0, 384, 128)
+    integral(192, 320, 0, 256, 256)
+    integral(192, 320, 256, 384, 128)
     y1[1].forward()
     x2[1].forward()
     for r in y1:
@@ -496,8 +498,8 @@
 
 
 def write(gamma_in, dens_in, gamma_ref, dens_ref, gamma_via, dens_via, sem):
-    parts = [(gamma_in.at[k, pl.ds(8 * r, 8)], gamma_via.at[k, pl.ds(8 * r, 8)], gamma_ref.at[k, pl.ds(8 * r, 8)])
-             for k in range(3) for r in range(3)] + [(dens_in, dens_via, dens_ref)]
+    spots = [(k, pl.ds(8 * r, 8), pl.ds(HALF * h, HALF)) for k in range(3) for r in range(3) for h in range(2)]
+    parts = [(gamma_in.at[p], gamma_via.at[p], gamma_ref.at[p]) for p in spots] + [(dens_in, dens_via, dens_ref)]
     come = [pltpu.make_async_copy(p[0], p[1], sem.at[0, n]) for n, p in enumerate(parts)]
     leave = [pltpu.make_async_copy(p[1], p[2], sem.at[1, n]) for n, p in enumerate(parts)]
     for cp in come:
@@ -542,7 +544,7 @@
     )(vir_energy.reshape(1, R), occ_energy.reshape(12, 128), pair_ids, b_factors)
     return pl.pallas_call(
         write, out_shape=shapes, in_specs=[anywhere, anywhere], out_specs=(anywhere, anywhere),
-        scratch_shapes=[V((3, R, 2 * HALF), F32), V((R, 16 * R), F32), pltpu.SemaphoreType.DMA((2, 10))], name="write",
+        scratch_shapes=[V((3, R, 2 * HALF), F32), V((R, 16 * R), F32), pltpu.SemaphoreType.DMA((2, 19))], name="write",
     )(gamma, density)
 
 

time: 145 us -> 145 us (level)
  no operation moved by 1% of the time
where the time goes in v5:
time: 145 us; the launch traced here: 143 us
  Pallas kernels  142 us (98%)
    pallas_call x1, Pallas kernels, shards(): pl.pallas_call(kernel, out_shape=shapes, in_specs=[vm, vm, pl.BlockSpec(m...  139 us

profile of v5, /device:TPU:33, one launch (start us, length us, event | category | flops | bytes accessed | tf_op | source)
XLA Modules:
  0.0 142.6 jit_solution(926302307767244481)
XLA Ops:
  0.6 139.1 %mp2.1 = (f32[3,24,8192]{2,1,0:T(8,128)}, f32[24,384]{1,0:T(8,128)}) custom-call(s32[1,24]{1,0:T(1,128)} %bitcast.3, s32[12,128]{1,0:T(8,128)} %bitcast.2, s32[3]{0:T(128)} %pid_ref.1, bf16[3,24,8192]{2,1,0:T(8,128)(2,1)} %b_hbm.1), custom_call_target="tpu_custom_call" | custom-call | flops 15000000512 | bytes 4000000 | tf_op jit(solution)/shard_map/mp2/pallas_call | solution.py:519
  139.8 2.7 %write.1 = (f32[3,24,8192]{2,1,0:T(8,128)}, f32[24,384]{1,0:T(8,128)}) custom-call(f32[3,24,8192]{2,1,0:T(8,128)} %get-tuple-element.4.gamma_in, f32[24,384]{1,0:T(8,128)} %get-tuple-element.5.dens_in), custom_call_target="tpu_custom_call" | custom-call | tf_op jit(solution)/shard_map/write/pallas_call | solution.py:545

commit v6 on v4

--- a/solution.py
+++ b/solution.py
@@ -264,25 +264,24 @@
     x2[1].forward()
     for r in y1:
         r.rest()
-    integral(0, 512, 384, 640, 256)
-    early = swapped(0, 512, 0, 640)
+    integral(0, 512, 384, 512, 128)
+    early = swapped(0, 512, 0, 512)
     x2[0].rest()
     x2[0].finish()
     y1[0].finish()
     early.wait_recv()
-    amplitude(0, 512, 0, 640)
+    amplitude(0, 512, 0, 512)
     x2[1].rest()
     x2[1].finish()
     y1[1].finish()
     integral(512, 256, 0, 512, 256)
-    integral(512, 256, 512, 640, 128)
-    late = [swapped(512, 256, 0, 640)]
-    integral(0, ROWS, 640, ROWS, 128)
-    late.append(swapped(0, ROWS, 640, ROWS))
+    late = [swapped(512, 256, 0, 512)]
+    integral(0, ROWS, 512, ROWS, 256)
+    late.append(swapped(0, ROWS, 512, ROWS))
     late[0].wait_recv()
-    amplitude(512, 256, 0, 640)
+    amplitude(512, 256, 0, 512)
     late[1].wait_recv()
-    amplitude(0, ROWS, 640, ROWS)
+    amplitude(0, ROWS, 512, ROWS)
 
     def store(t, h, n, cs, out, acc, hold, l, d):
         acc[t, h, :, cs] = out[0:n]

time: 145 us -> 144 us (level)
  no operation moved by 1% of the time
where the time goes in v6:
time: 144 us; the launch traced here: 142 us
  Pallas kernels  142 us (99%)
    pallas_call x1, Pallas kernels, shards(): pl.pallas_call(kernel, out_shape=shapes, in_specs=[vm, vm, pl.BlockSpec(m...  139 us

profile of v6, /device:TPU:33, one launch (start us, length us, event | category | flops | bytes accessed | tf_op | source)
XLA Modules:
  0.0 142.5 jit_solution(7427509850268134665)
XLA Ops:
  0.6 139.2 %mp2.1 = (f32[3,24,8192]{2,1,0:T(8,128)}, f32[24,384]{1,0:T(8,128)}) custom-call(s32[1,24]{1,0:T(1,128)} %bitcast.3, s32[12,128]{1,0:T(8,128)} %bitcast.2, s32[3]{0:T(128)} %pid_ref.1, bf16[3,24,8192]{2,1,0:T(8,128)(2,1)} %b_hbm.1), custom_call_target="tpu_custom_call" | custom-call | flops 15000000512 | bytes 4000000 | tf_op jit(solution)/shard_map/mp2/pallas_call | solution.py:516
  139.8 2.5 %write.1 = (f32[3,24,8192]{2,1,0:T(8,128)}, f32[24,384]{1,0:T(8,128)}) custom-call(f32[3,24,8192]{2,1,0:T(8,128)} %get-tuple-element.4.gamma_in, f32[24,384]{1,0:T(8,128)} %get-tuple-element.5.dens_in), custom_call_target="tpu_custom_call" | custom-call | tf_op jit(solution)/shard_map/write/pallas_call | solution.py:542
